TPU v7x, 32 devices: a whole 2x2x4 slice. The times are simulated.
32 devices in a mesh: groups: 2 (over y), tm: 4 (over z), space: 2 (over x), clip: 2 (over core).
Axes of the slice: x: 2, y: 2, z: 4, core: 2. Of those that a mesh axis runs over, the one named last changes fastest.
Arguments:
- latents: bfloat16 [4, 16, 8, 6144], P(('groups', 'clip'), 'tm', 'space'), parts along dimension 0, may hold values from -6 to 6
- frame_counts: int32 [4], P(('groups', 'clip')), parts along dimension 0, may hold values from 2 to 16, as said below
- gain_first: float32 [192], replicated, may hold values from 0.5 to 1.5
- bias_first: float32 [192], replicated, may hold values from -3 to 3
- weight_first: bfloat16 [3, 3, 3, 192, 192], replicated, may hold values from -0.078125 to 0.078125
- gain_second: float32 [192], replicated, may hold values from 0.5 to 1.5
- bias_second: float32 [192], replicated, may hold values from -3 to 3
- weight_second: bfloat16 [3, 3, 3, 192, 192], replicated, may hold values from -0.078125 to 0.078125
Outputs:
- encoded: bfloat16 [4, 16, 8, 6144], P(('groups', 'clip'), 'tm', 'space'), parts along dimension 0
There are 2 independent parts, one for each index of `groups`. A program takes and returns all parts, laid end to end along the dimension named above; an argument that names none is the same for every part. Nothing has to cross between parts.
Inputs may be any that keep to these rules, and one draw needn't show every extreme that they name: `frame_counts`: in every part exactly one clip has all 16 frames valid; every other clip has fewer.
All inputs are finite; a program needn't handle non-finite values.
Results may differ from a plain program's by a relative error of at most 0.007.
Values may be sent and summed in bfloat16 or wider, within the bound.
A program may use at most 64 MiB of HBM per device.

v0:
```python
import functools

import jax
import jax.numpy as jnp
from jax import lax
from jax.experimental import pallas as pl
from jax.experimental.pallas import tpu as pltpu
from jax.sharding import PartitionSpec as P

MESH = pl.DeviceIdType.MESH
WIDE = 256


def pair_norm(values, valid, gain):
    channels = gain.shape[-1]
    mean_square = jnp.sum(values * values, axis=-1, keepdims=True) * (1.0 / channels)
    scaled = values * lax.rsqrt(mean_square + 1e-06) * gain
    out = scaled * jax.nn.sigmoid(scaled)
    return jnp.where(valid, out, 0.0)


def split_pair(flat, channels):
    return flat[..., :channels], flat[..., channels:]


def kernel(
    bands,
    blocks,
    counts_ref,
    x_ref,
    gain1_hbm,
    bias1_hbm,
    gain2_hbm,
    bias2_hbm,
    w1_ref,
    w2_ref,
    out_ref,
    vectors,
    w1,
    w2,
    p1,
    p2,
    from_time,
    from_space,
    from_corner,
    hidden_out,
    hidden_in,
    w_sems,
    send_sems,
    recv_sems,
):
    frames, rows, pairs, flat = x_ref.shape
    channels = flat // 2
    sides = 1 if bands == 2 else 2
    extra = sides
    hrows = rows + extra
    tm = lax.axis_index("tm")
    band = lax.axis_index("space")
    has_prev = tm > 0
    has_next = tm < blocks - 1
    count = counts_ref[0]
    if sides == 1:
        other = 1 - band
        links = [(other, None, other * (rows - 2), 0)]
        own_at = 1 + band
        slot_at = [(1 - band) * (rows + 1)]
        hidden_at = 1 - band
    else:
        links = [
            (band - 1, band > 0, 0, 1),
            (band + 1, band < bands - 1, rows - 2, 0),
        ]
        own_at = 2
        slot_at = [0, rows + 2]
        hidden_at = 0

    def both(a, b):
        return b if a is None else (a if b is None else jnp.logical_and(a, b))

    def when(cond, fn):
        if cond is None:
            fn()
        else:
            pl.when(cond)(fn)

    peers = [({"space": p}, c) for p, c, _, _ in links]
    for step, has in ((1, has_next), (-1, has_prev)):
        peers.append(({"tm": tm + step}, has))
        peers += [({"tm": tm + step, "space": p}, both(c, has)) for p, c, _, _ in links]

    barrier = pltpu.get_barrier_semaphore()
    total = 0
    for device, cond in peers:
        when(
            cond,
            lambda device=device: pl.semaphore_signal(
                barrier, inc=1, device_id=device, device_id_type=MESH
            ),
        )
        total = total + (1 if cond is None else cond.astype(jnp.int32))

    load1 = pltpu.make_async_copy(w1_ref, w1.at[:, pl.ds(0, channels)], w_sems.at[0])
    load2 = pltpu.make_async_copy(w2_ref, w2.at[:, pl.ds(0, channels)], w_sems.at[1])
    small = [
        pltpu.make_async_copy(source, vectors.at[i], w_sems.at[2 + i])
        for i, source in enumerate((gain1_hbm, bias1_hbm, gain2_hbm, bias2_hbm))
    ]
    gain1_ref, bias1_ref, gain2_ref, bias2_ref = [vectors.at[i] for i in range(4)]
    for copy in small:
        copy.start()
    load1.start()
    load2.start()

    p1[...] = jnp.zeros_like(p1)
    p2[...] = jnp.zeros_like(p2)
    spare = WIDE - channels
    w1[:, channels:] = jnp.zeros((w1.shape[0], spare, channels), w1.dtype)
    w2[:, channels:] = jnp.zeros((w2.shape[0], spare, channels), w2.dtype)

    pl.semaphore_wait(barrier, total)

    tail = pl.ds(frames - 2, 2)
    copies = []

    def remote(src, dst, at, device, send_if, recv_if):
        copy = pltpu.make_async_remote_copy(
            src_ref=src,
            dst_ref=dst,
            send_sem=send_sems.at[at],
            recv_sem=recv_sems.at[at],
            device_id=device,
            device_id_type=MESH,
        )
        return copy, send_if, recv_if

    slot_cond = [None] if sides == 1 else [band > 0, band < bands - 1]
    space_copies, corner_copies = [], []
    for peer, cond, edge, slot in links:
        space_copies.append(
            remote(
                x_ref.at[:, pl.ds(edge, 2)], from_space.at[slot], slot, {"space": peer}, cond, None
            )
        )
        corner_copies.append(
            remote(
                x_ref.at[tail, pl.ds(edge, 2)],
                from_corner.at[slot],
                2 + slot,
                {"tm": tm + 1, "space": peer},
                both(cond, has_next),
                None,
            )
        )
    time_copy = remote(x_ref.at[tail], from_time, 4, {"tm": tm + 1}, has_next, has_prev)
    hidden_copy = remote(hidden_out, hidden_in, 5, {"tm": tm + 1}, has_next, has_prev)
    for copy, cond, _ in space_copies + [time_copy] + corner_copies:
        when(cond, copy.start)

    first = tm * frames
    pair_index = lax.broadcasted_iota(jnp.int32, (1, 1, pairs, 1), 2)

    def put(planes, even, odd, frame_at, row_at):
        nf, nr = even.shape[:2]
        before = jnp.where(pair_index > 0, pltpu.roll(odd, 1, 2), 0.0)
        after = jnp.where(pair_index < pairs - 1, pltpu.roll(even, pairs - 1, 2), 0.0)
        for plane, values in enumerate((before, even, odd, after)):
            planes[plane, pl.ds(frame_at, nf), pl.ds(row_at, nr), :, pl.ds(0, channels)] = (
                values.astype(planes.dtype)
            )

    def frame_valid(shape, frame_at):
        index = first - 2 + frame_at + lax.broadcasted_iota(jnp.int32, shape, 0)
        return index < count

    def put_input(raw, frame_at, row_at):
        nf, nr = raw.shape[:2]
        even, odd = split_pair(raw.astype(jnp.float32), channels)
        valid = frame_valid((nf, 1, 1, 1), frame_at)
        gain = gain1_ref[...].reshape(1, 1, 1, channels)
        put(p1, pair_norm(even, valid, gain), pair_norm(odd, valid, gain), frame_at, row_at)

    def conv(planes, w, frame_at, nf, nr, row_at=0):
        total = None
        for a in range(3):
            for b in range(3):
                for e in range(3):
                    patch = planes[
                        e : e + 2, frame_at + a : frame_at + a + nf, pl.ds(row_at + b, nr)
                    ].reshape(2 * nf * nr * pairs, WIDE)
                    term = jnp.dot(
                        patch, w[(a * 3 + b) * 3 + e], preferred_element_type=jnp.float32
                    )
                    total = term if total is None else total + term
        return total.reshape(2, nf, nr, pairs, channels)

    def hidden(frame_at, nf, nr=hrows, row_at=0):
        summed = conv(p1, w1, frame_at, nf, nr, row_at) + bias1_ref[...].reshape(1, 1, 1, 1, channels)
        valid = frame_valid((nf, 1, 1, 1), frame_at + 2)
        if sides == 2:
            row = band * rows - 1 + lax.broadcasted_iota(jnp.int32, (1, hrows, 1, 1), 1)
            valid = valid & (row >= 0) & (row < bands * rows)
        rounded = summed.astype(jnp.bfloat16).astype(jnp.float32)
        gain = gain2_ref[...].reshape(1, 1, 1, channels)
        even = pair_norm(rounded[0], valid, gain)
        odd = pair_norm(rounded[1], valid, gain)
        put(p2, even, odd, frame_at + 2, hidden_at + row_at)
        return jnp.concatenate([even, odd], axis=-1).astype(hidden_out.dtype)

    def finish(frame_at, nf):
        summed = conv(p2, w2, frame_at, nf, rows) + bias2_ref[...].reshape(1, 1, 1, 1, channels)
        joined = jnp.concatenate([summed[0], summed[1]], axis=-1)
        added = joined + x_ref[pl.ds(frame_at, nf)].astype(jnp.float32)
        valid = frame_valid((nf, 1, 1, 1), frame_at + 2)
        out_ref[pl.ds(frame_at, nf)] = jnp.where(valid, added, 0.0).astype(out_ref.dtype)

    for copy in small:
        copy.wait()
    put_input(x_ref[...], 2, own_at)
    load1.wait()
    if sides == 1:
        near = rows - 1
        hidden_out[:, pl.ds(2 * band, near)] = hidden(frames - 2, 2, near, 2 * band)
    for slot, (copy, _, _) in enumerate(space_copies):

        def arrived(slot=slot):
            landed = remote(
                x_ref.at[:, pl.ds(0, 2)], from_space.at[slot], slot, {"space": band}, None, None
            )[0]
            landed.wait_recv()
            put_input(from_space[slot], 2, slot_at[slot])

        when(slot_cond[slot], arrived)

    if sides == 1:
        far_at = near * (1 - band)
        hidden_out[:, pl.ds(far_at, 2)] = hidden(frames - 2, 2, 2, far_at)
    else:
        hidden_out[...] = hidden(frames - 2, 2)
    when(has_next, hidden_copy[0].start)

    def time_arrived():
        time_copy[0].wait_recv()
        put_input(from_time[...], 0, own_at)

    when(has_prev, time_arrived)
    for slot in range(sides):

        def corner_arrived(slot=slot):
            landed = remote(
                x_ref.at[tail, pl.ds(0, 2)],
                from_corner.at[slot],
                2 + slot,
                {"space": band},
                None,
                None,
            )[0]
            landed.wait_recv()
            put_input(from_corner[slot], 0, slot_at[slot])

        when(both(slot_cond[slot], has_prev), corner_arrived)

    hidden(0, frames - 2)
    load2.wait()
    finish(frames - 2, 2)

    def hidden_arrived():
        hidden_copy[0].wait_recv()
        even, odd = split_pair(hidden_in[...].astype(jnp.float32), channels)
        put(p2, even, odd, 0, hidden_at)

    when(has_prev, hidden_arrived)
    finish(0, frames - 2)
    for copy, cond, _ in space_copies + corner_copies + [time_copy, hidden_copy]:
        when(cond, copy.wait_send)


def shards(
    bands,
    blocks,
    latents,
    frame_counts,
    gain_first,
    bias_first,
    weight_first,
    gain_second,
    bias_second,
    weight_second,
):
    channels = gain_first.shape[0]
    frames, rows, flat_width = latents.shape[1:]
    pairs = flat_width // (2 * channels)
    x = latents.reshape(frames, rows, pairs, 2 * channels)
    sides = 1 if bands == 2 else 2
    hrows = rows + sides
    bf16 = jnp.bfloat16
    vmem = pl.BlockSpec(memory_space=pltpu.VMEM)
    hbm = pl.BlockSpec(memory_space=pltpu.HBM)
    out = pl.pallas_call(
        functools.partial(kernel, bands, blocks),
        out_shape=pltpu.VMEM(x.shape, bf16),
        in_specs=[pl.BlockSpec(memory_space=pltpu.SMEM)] + [vmem] + [hbm] * 6,
        out_specs=vmem,
        scratch_shapes=[
            pltpu.VMEM((4, 1, channels), jnp.float32),
            pltpu.VMEM((27, WIDE, channels), bf16),
            pltpu.VMEM((27, WIDE, channels), bf16),
            pltpu.VMEM((4, frames + 2, hrows + 2, pairs, WIDE), bf16),
            pltpu.VMEM((4, frames + 2, rows + 2, pairs, WIDE), bf16),
            pltpu.VMEM((2, rows, pairs, 2 * channels), bf16),
            pltpu.VMEM((sides, frames, 2, pairs, 2 * channels), bf16),
            pltpu.VMEM((sides, 2, 2, pairs, 2 * channels), bf16),
            pltpu.VMEM((2, hrows, pairs, 2 * channels), bf16),
            pltpu.VMEM((2, hrows, pairs, 2 * channels), bf16),
            pltpu.SemaphoreType.DMA((6,)),
            pltpu.SemaphoreType.DMA((6,)),
            pltpu.SemaphoreType.DMA((6,)),
        ],
        compiler_params=pltpu.CompilerParams(
            collective_id=0, has_side_effects=True, vmem_limit_bytes=40 * 1024 * 1024
        ),
    )(
        frame_counts,
        pltpu.with_memory_space_constraint(x, pltpu.VMEM),
        pltpu.with_memory_space_constraint(gain_first.reshape(1, channels), pltpu.HBM),
        pltpu.with_memory_space_constraint(bias_first.reshape(1, channels), pltpu.HBM),
        pltpu.with_memory_space_constraint(gain_second.reshape(1, channels), pltpu.HBM),
        pltpu.with_memory_space_constraint(bias_second.reshape(1, channels), pltpu.HBM),
        pltpu.with_memory_space_constraint(weight_first.reshape(27, channels, channels), pltpu.HBM),
        pltpu.with_memory_space_constraint(weight_second.reshape(27, channels, channels), pltpu.HBM),
    )
    return out.reshape(latents.shape)


def solution(mesh):
    return jax.shard_map(
        functools.partial(shards, mesh.shape["space"], mesh.shape["tm"]),
        mesh=mesh,
        in_specs=(P(("groups", "clip"), "tm", "space", None), P(("groups", "clip"))) + (P(),) * 6,
        out_specs=P(("groups", "clip"), "tm", "space", None),
        check_vma=False,
    )
```

profile of v0, /device:TPU:14, one launch (start us, length us, event | category | flops | bytes accessed | tf_op | source)
XLA Modules:
  0.0 17.3 jit_solution(6519777912198181531)
XLA Ops:
  0.7 1.1 %reshape.24.x_ref = bf16[4,4,16,384]{3,2,1,0:T(8,128)(2,1)S(1)} reshape(bf16[1,4,4,6144]{3,2,1,0:T(4,128)(2,1)} %param.8) | data formatting | bytes 393216 | tf_op jit(solution)/shard_map/reshape | solution.py:292
  1.7 14.9 %shard_map.82 = bf16[4,4,16,384]{3,2,1,0:T(8,128)(2,1)S(1)} custom-call(s32[1]{0:T(128)S(6)} %copy.9.counts_ref, bf16[4,4,16,384]{3,2,1,0:T(8,128)(2,1)S(1)} %reshape.24.x_ref, f32[1,192]{1,0:T(1,128)} %bitcast.10, f32[1,192]{1,0:T(1,128)} %bitcast.11, f32[1,192]{1,0:T(1,128)} %bitcast.12, f32[1,192]{1,0:T(1,128)} %bitcast.13, ...), custom_call_target="tpu_custom_call" | custom-call | tf_op jit(solution)/shard_map/pallas_call | solution.py:298
  16.6 0.7 %reshape.31 = bf16[1,4,4,6144]{3,2,1,0:T(4,128)(2,1)} reshape(bf16[4,4,16,384]{3,2,1,0:T(8,128)(2,1)S(1)} %shard_map.82) | data formatting | bytes 393216 | tf_op jit(solution)/shard_map/reshape | solution.py:331
where the time goes:
time: 17.5 us; the launch traced here: 17.3 us
  Pallas kernels  14.9 us (85%)
  local copies, waits for them, and re-layouts  1.78 us (10%)
  between operations  0.66 us (4%)
    pallas_call x1, Pallas kernels, shards(): pl.pallas_call(functools.partial(kernel, bands, blocks), out_shape=pltpu....  14.9 us
    reshape x1, local copies, waits for them, and re-layouts, shards(): x = latents.reshape(frames, rows, pairs, 2 * channels)  1.05 us
    reshape x1, local copies, waits for them, and re-layouts, shards(): return out.reshape(latents.shape)  0.73 us

commit v1 on v0

v1 whole, which is shorter than its diff:
```python
import functools

import jax
import jax.numpy as jnp
from jax import lax
from jax.experimental import pallas as pl
from jax.experimental.pallas import tpu as pltpu
from jax.sharding import PartitionSpec as P

MESH = pl.DeviceIdType.MESH
LANES = 128
BF16 = jnp.bfloat16
F32 = jnp.float32


def kernel(
    bands,
    blocks,
    counts_ref,
    x_hbm,
    gain1_hbm,
    bias1_hbm,
    gain2_hbm,
    bias2_hbm,
    w1_hbm,
    w2_hbm,
    out_ref,
    vectors,
    w1,
    w2,
    x_ref,
    p1,
    p2,
    own,
    halo,
    tail,
    corner,
    early,
    from_time,
    from_space,
    from_corner,
    hidden_out,
    hidden_in,
    l_sems,
    send_sems,
    recv_sems,
):
    frames, rows, width = x_ref.shape
    channels = vectors.shape[-1]
    flat = 2 * channels
    pairs = width // flat
    half = flat // 2 - LANES
    sides = 1 if bands == 2 else 2
    first_hidden = 0 if sides == 1 else -1
    hrows = rows + sides
    base1 = 1 if sides == 1 else 2
    tm = lax.axis_index("tm")
    band = lax.axis_index("space")
    has_prev = tm > 0
    has_next = tm < blocks - 1
    count = counts_ref[0]

    def both(a, b):
        return b if a is None else (a if b is None else jnp.logical_and(a, b))

    def when(cond, fn):
        if cond is None:
            fn()
        else:
            pl.when(cond)(fn)

    if sides == 1:
        flip = band
        links = [(1 - band, None, (1 - band) * (rows - 2), 0)]
        slot_cond = [None]
    else:
        flip = 0
        links = [
            (band - 1, band > 0, 0, 1),
            (band + 1, band < bands - 1, rows - 2, 0),
        ]
        slot_cond = [band > 0, band < bands - 1]

    peers = [({"space": p}, c) for p, c, _, _ in links]
    for step, has in ((1, has_next), (-1, has_prev)):
        peers.append(({"tm": tm + step}, has))
        peers += [({"tm": tm + step, "space": p}, both(c, has)) for p, c, _, _ in links]

    barrier = pltpu.get_barrier_semaphore()
    total = 0
    for device, cond in peers:
        when(
            cond,
            lambda device=device: pl.semaphore_signal(
                barrier, inc=1, device_id=device, device_id_type=MESH
            ),
        )
        total = total + (1 if cond is None else cond.astype(jnp.int32))

    load_x = pltpu.make_async_copy(x_hbm, x_ref, l_sems.at[0])
    loads = []
    for n, (source, target) in enumerate(((w1_hbm, w1), (w2_hbm, w2))):
        loads.append(
            [
                pltpu.make_async_copy(
                    source.at[:, b + flip * (2 - 2 * b)], target.at[:, b], l_sems.at[1 + 3 * n + b]
                )
                for b in range(3)
            ]
        )
    small = [
        pltpu.make_async_copy(source, vectors.at[i], l_sems.at[7 + i])
        for i, source in enumerate((gain1_hbm, bias1_hbm, gain2_hbm, bias2_hbm))
    ]
    load_x.start()
    for copy in small:
        copy.start()
    for copy in loads[0] + loads[1]:
        copy.start()

    def fill(ref):
        ref[...] = jnp.zeros(ref.shape, ref.dtype)

    pad = jnp.zeros((frames + 2, 1) + p1.shape[2:], BF16)
    if sides == 1:
        p1[:, 0:1] = pad
        p2[:, 0:1] = pad

    def no_prev():
        fill(from_time)
        fill(from_corner)
        for ref in hidden_in:
            fill(ref)

    pl.when(jnp.logical_not(has_prev))(no_prev)
    if sides == 2:
        for slot in range(2):

            def outside(slot=slot):
                from_space[slot] = jnp.zeros(from_space.shape[1:], BF16)

            def outside_corner(slot=slot):
                from_corner[slot] = jnp.zeros(from_corner.shape[1:], BF16)

            pl.when(jnp.logical_not(slot_cond[slot]))(outside)
            pl.when(jnp.logical_and(jnp.logical_not(slot_cond[slot]), has_prev))(outside_corner)

    load_x.wait()
    pl.semaphore_wait(barrier, total)

    def remote(src, dst, at, device):
        return pltpu.make_async_remote_copy(
            src_ref=src,
            dst_ref=dst,
            send_sem=send_sems.at[at],
            recv_sem=recv_sems.at[at],
            device_id=device,
            device_id_type=MESH,
        )

    last = pl.ds(frames - 2, 2)
    sends = []
    for peer, cond, edge, slot in links:
        copy = remote(x_ref.at[:, pl.ds(edge, 2)], from_space.at[slot], slot, {"space": peer})
        sends.append((copy, cond))
    time_copy = remote(x_ref.at[last], from_time, 4, {"tm": tm + 1})
    sends.append((time_copy, has_next))
    for peer, cond, edge, slot in links:
        copy = remote(
            x_ref.at[last, pl.ds(edge, 2)],
            from_corner.at[slot],
            2 + slot,
            {"tm": tm + 1, "space": peer},
        )
        sends.append((copy, both(cond, has_next)))
    for copy, cond in sends:
        when(cond, copy.start)

    first = tm * frames
    lane = lax.broadcasted_iota(jnp.int32, (pairs, LANES), 1)
    pair = lax.broadcasted_iota(jnp.int32, (pairs, LANES), 0)
    low = lane < half

    def wide(i):
        value = vectors[i]
        return jnp.concatenate([value, value], axis=-1)

    def scale_of(gain, frame_at):
        return gain * jnp.where(first - 2 + frame_at < count, 1.0, 0.0)

    def natural(row, size):
        if sides == 2:
            return row
        return row + flip * (size - 1 - 2 * row)

    def spread(source, rows_in, target):
        for p in range(pairs):
            for i in range(3):
                at = p * flat + i * LANES
                part = source[:, at : at + LANES].astype(F32)
                target.at[i][pl.ds(p, rows_in, stride=pairs), :] = part

    def row_at(ref, row, size):
        start = natural(row, size) * pairs
        if not isinstance(start, int):
            start = pl.multiple_of(start, pairs)
        return jnp.concatenate([ref[i, pl.ds(start, pairs), :] for i in range(3)], axis=-1)

    def before(v):
        return jnp.where(pair > 0, pltpu.roll(v, 1, 0), 0.0)

    def after(v):
        return jnp.where(pair < pairs - 1, pltpu.roll(v, pairs - 1, 0), 0.0)

    def put(plane, tiles, frame_at, row_index, with_tiles=True):
        v0, v1, v2 = tiles
        mixed = jnp.where(low, after(v1), before(v1))
        for i, v in enumerate((v0, v1, v2, after(v0), before(v2), mixed)):
            plane[frame_at, row_index, :, i * LANES : (i + 1) * LANES] = v.astype(BF16)

    def tiles_of(value):
        return [value[:, i * LANES : (i + 1) * LANES] for i in range(3)]

    def norm(value, scale):
        v0, v1, v2 = tiles_of(value)
        s1 = v1 * v1
        even = jnp.sum(v0 * v0 + jnp.where(low, s1, 0.0), axis=-1, keepdims=True)
        odd = jnp.sum(v2 * v2 + jnp.where(low, 0.0, s1), axis=-1, keepdims=True)
        even = lax.rsqrt(even * (1.0 / channels) + 1e-06)
        odd = lax.rsqrt(odd * (1.0 / channels) + 1e-06)
        out = []
        for i, (v, inverse) in enumerate(((v0, even), (v1, jnp.where(low, even, odd)), (v2, odd))):
            scaled = v * inverse * scale[:, i * LANES : (i + 1) * LANES]
            out.append(scaled * jax.nn.sigmoid(scaled))
        return out

    def conv(plane, w, frame_at, nf, row_index, nr, taps):
        even, odd = None, None

        def add(acc, lhs, rhs):
            term = jnp.dot(lhs, rhs, preferred_element_type=F32)
            return term if acc is None else acc + term

        rest = LANES - half
        zero = jnp.zeros((half, channels), BF16)
        held = []
        for a in taps:
            for b in range(3):

                def tile(i, n=1, a=a, b=b):
                    value = plane[
                        frame_at + a : frame_at + a + nf,
                        row_index + b : row_index + b + nr,
                        :,
                        i * LANES : (i + n) * LANES,
                    ]
                    return value.reshape(nf * nr * pairs, n * LANES)

                k0, k1, k2 = [w.at[a, b, e] for e in range(3)]
                main = tile(0, 2)
                third = tile(2)
                even = add(even, main, jnp.concatenate([k1[...], k2[:half]], axis=0))
                odd = add(odd, main, jnp.concatenate([k0[...], k1[:half]], axis=0))
                even = add(
                    even,
                    jnp.concatenate([third, tile(4)], axis=-1),
                    jnp.concatenate([k2[half:], k0[half:]], axis=0),
                )
                odd = add(
                    odd,
                    jnp.concatenate([third, tile(3)], axis=-1),
                    jnp.concatenate([k1[half:], k2[:LANES]], axis=0),
                )
                held.append((tile(5), [zero, k0[:half]], [k2[LANES:], zero]))
                if len(held) == 2 or (a == taps[-1] and b == 2):
                    lhs = jnp.concatenate([h[0] for h in held], axis=-1)
                    even = add(even, lhs, jnp.concatenate(sum([h[1] for h in held], []), axis=0))
                    odd = add(odd, lhs, jnp.concatenate(sum([h[2] for h in held], []), axis=0))
                    held = []
        return jnp.concatenate([even, odd], axis=-1)

    def piece(value, n):
        return value[n * pairs : (n + 1) * pairs]

    def put_rows(source, rows_in, target, frame_at, row_list):
        spread(source, rows_in, target)
        scale = scale_of(gain1, frame_at)
        for row, row_index in row_list:
            put(p1, norm(row_at(target, row, rows_in), scale), frame_at, row_index)

    def hidden(frame_at, nf, row, nr, saved=None):
        summed = conv(p1, w1, frame_at, nf, row - 1 + base1, nr, (0, 1, 2)) + bias1
        rounded = summed.astype(BF16).astype(F32)
        for f in range(nf):
            scale = scale_of(gain2, frame_at + f + 2)
            for r in range(nr):
                at = row + r
                inside = scale
                if sides == 2 and (at < 0 or at >= rows):
                    inside = scale * jnp.where(slot_cond[0 if at < 0 else 1], 1.0, 0.0)
                tiles = norm(piece(rounded, f * nr + r), inside)
                put(p2, tiles, frame_at + f + 2, at + 1)
                if saved is not None:
                    for i, v in enumerate(tiles):
                        saved[f, r, :, i * LANES : (i + 1) * LANES] = v.astype(BF16)

    def settle(f, values):
        valid = jnp.where(first + f < count, 1.0, 0.0)
        for r in range(rows):
            start = natural(r, rows) * pairs
            if not isinstance(start, int):
                start = pl.multiple_of(start, pairs)
            for i, v in enumerate(tiles_of(values[r] * valid)):
                own[f, i, pl.ds(start, pairs), :] = v
        for p in range(pairs):
            for i in range(3):
                value = own.at[f, i][pl.ds(p, rows, stride=pairs), :]
                at = p * flat + i * LANES
                out_ref[f, :, at : at + LANES] = value.astype(BF16)

    def with_input(f, summed):
        return [piece(summed, r) + row_at(own.at[f], r, rows) for r in range(rows)]

    for copy in small:
        copy.wait()
    gain1, bias1, gain2, bias2 = [wide(i) for i in range(4)]
    for f in range(frames):
        put_rows(x_ref.at[f], rows, own.at[f], f + 2, [(r, r + base1) for r in range(rows)])
    for copy in loads[0]:
        copy.wait()
    hidden_copies = []
    if sides == 1:
        parts = [(0, rows - 1), (rows - 1, 2)]
    else:
        parts = [(first_hidden, hrows)]
    for n in range(len(parts)):
        hidden_copies.append(remote(hidden_out[n], hidden_in[n], 5 + n, {"tm": tm + 1}))
    if sides == 1:
        hidden(frames - 2, 2, *parts[0], hidden_out[0])
        when(has_next, hidden_copies[0].start)

    def halo_rows(slot):
        if sides == 1:
            return [(0, rows + base1), (1, rows + 1 + base1)]
        at = 0 if slot == 0 else rows + 2
        return [(0, at), (1, at + 1)]

    for slot in range(sides):
        landed = remote(
            x_ref.at[:, pl.ds(0, 2)], from_space.at[slot], slot, {"space": band}
        )
        when(slot_cond[slot], landed.wait_recv)
        for f in range(frames):
            put_rows(from_space.at[slot, f], 2, halo.at[slot, f], f + 2, halo_rows(slot))
    hidden(frames - 2, 2, *parts[-1], hidden_out[-1])
    when(has_next, hidden_copies[-1].start)

    pl.when(has_prev)(time_copy.wait_recv)
    for slot in range(sides):
        landed = remote(
            x_ref.at[last, pl.ds(0, 2)], from_corner.at[slot], 2 + slot, {"space": band}
        )
        when(both(slot_cond[slot], has_prev), landed.wait_recv)
    for f in range(2):
        put_rows(from_time.at[f], rows, tail.at[f], f, [(r, r + base1) for r in range(rows)])
        for slot in range(sides):
            put_rows(from_corner.at[slot, f], 2, corner.at[slot, f], f, halo_rows(slot))

    hidden(0, frames - 2, first_hidden, hrows)
    for copy in loads[1]:
        copy.wait()
    summed = conv(p2, w2, frames - 2, 2, 0, rows, (0, 1, 2)) + bias2
    for f in range(2):
        settle(
            frames - 2 + f,
            with_input(frames - 2 + f, summed[f * rows * pairs : (f + 1) * rows * pairs]),
        )
    for f, taps in ((0, (2,)), (1, (1, 2))):
        values = with_input(f, conv(p2, w2, f, 1, 0, rows, taps) + bias2)
        for r in range(rows):
            early[f, r] = values[r]

    for copy in hidden_copies:
        pl.when(has_prev)(copy.wait_recv)
    for (row, nr), ref in zip(parts, hidden_in):
        for f in range(2):
            for r in range(nr):
                put(p2, tiles_of(ref[f, r].astype(F32)), f, row + r + 1)
    for f, taps in ((0, (0, 1)), (1, (0,))):
        summed = conv(p2, w2, f, 1, 0, rows, taps)
        settle(f, [piece(summed, r) + early[f, r] for r in range(rows)])
    for copy, cond in sends + [(c, has_next) for c in hidden_copies]:
        when(cond, copy.wait_send)


def shards(
    bands,
    blocks,
    latents,
    frame_counts,
    gain_first,
    bias_first,
    weight_first,
    gain_second,
    bias_second,
    weight_second,
):
    channels = gain_first.shape[0]
    frames, rows, width = latents.shape[1:]
    flat = 2 * channels
    pairs = width // flat
    x = latents.reshape(frames, rows, width)
    sides = 1 if bands == 2 else 2
    vmem = pl.BlockSpec(memory_space=pltpu.VMEM)
    hbm = pl.BlockSpec(memory_space=pltpu.HBM)
    parts = [rows - 1, 2] if sides == 1 else [rows + 2]
    scratch = pltpu.VMEM
    rows1 = rows + (3 if sides == 1 else 4)
    out = pl.pallas_call(
        functools.partial(kernel, bands, blocks),
        out_shape=pltpu.VMEM(x.shape, BF16),
        in_specs=[pl.BlockSpec(memory_space=pltpu.SMEM)] + [hbm] * 7,
        out_specs=vmem,
        scratch_shapes=[
            scratch((4, 1, channels), F32),
            scratch((3, 3, 3, channels, channels), BF16),
            scratch((3, 3, 3, channels, channels), BF16),
            scratch(x.shape, BF16),
            scratch((frames + 2, rows1, pairs, 6 * LANES), BF16),
            scratch((frames + 2, rows + 2, pairs, 6 * LANES), BF16),
            scratch((frames, 3, rows * pairs, LANES), F32),
            scratch((sides, frames, 3, 2 * pairs, LANES), F32),
            scratch((2, 3, rows * pairs, LANES), F32),
            scratch((sides, 2, 3, 2 * pairs, LANES), F32),
            scratch((2, rows, pairs, flat), F32),
            scratch((2, rows, width), BF16),
            scratch((sides, frames, 2, width), BF16),
            scratch((sides, 2, 2, width), BF16),
            [scratch((2, n, pairs, flat), BF16) for n in parts],
            [scratch((2, n, pairs, flat), BF16) for n in parts],
            pltpu.SemaphoreType.DMA((11,)),
            pltpu.SemaphoreType.DMA((7,)),
            pltpu.SemaphoreType.DMA((7,)),
        ],
        compiler_params=pltpu.CompilerParams(
            collective_id=0, has_side_effects=True, vmem_limit_bytes=40 * 1024 * 1024
        ),
    )(
        frame_counts,
        pltpu.with_memory_space_constraint(x, pltpu.HBM),
        pltpu.with_memory_space_constraint(gain_first.reshape(1, channels), pltpu.HBM),
        pltpu.with_memory_space_constraint(bias_first.reshape(1, channels), pltpu.HBM),
        pltpu.with_memory_space_constraint(gain_second.reshape(1, channels), pltpu.HBM),
        pltpu.with_memory_space_constraint(bias_second.reshape(1, channels), pltpu.HBM),
        pltpu.with_memory_space_constraint(weight_first, pltpu.HBM),
        pltpu.with_memory_space_constraint(weight_second, pltpu.HBM),
    )
    return out.reshape(latents.shape)


def solution(mesh):
    return jax.shard_map(
        functools.partial(shards, mesh.shape["space"], mesh.shape["tm"]),
        mesh=mesh,
        in_specs=(P(("groups", "clip"), "tm", "space", None), P(("groups", "clip"))) + (P(),) * 6,
        out_specs=P(("groups", "clip"), "tm", "space", None),
        check_vma=False,
    )
```

time: 17.5 us -> 14.9 us (0.85)
  the two profiles are of different devices: /device:TPU:14 before, /device:TPU:0 now
where the time goes in v1:
time: 14.9 us; the launch traced here: 14.7 us
  Pallas kernels  13.4 us (90%)
  local copies, waits for them, and re-layouts  0.68 us (5%)
  between operations  0.66 us (4%)
    pallas_call x1, Pallas kernels, shards(): pl.pallas_call(functools.partial(kernel, bands, blocks), out_shape=pltpu....  13.4 us
    unnamed x1, local copies, waits for them, and re-layouts  0.68 us

profile of v1, /device:TPU:0, one launch (start us, length us, event | category | flops | bytes accessed | tf_op | source)
XLA Modules:
  0.0 14.7 jit_solution(14273046421478441592)
XLA Ops:
  0.7 13.4 %shard_map.82 = bf16[4,4,6144]{2,1,0:T(4,128)(2,1)S(1)} custom-call(s32[1]{0:T(128)S(6)} %copy.11.counts_ref, bf16[4,4,6144]{2,1,0:T(4,128)(2,1)} %bitcast.7, f32[1,192]{1,0:T(1,128)} %bitcast.8, f32[1,192]{1,0:T(1,128)} %bitcast.9, f32[1,192]{1,0:T(1,128)} %bitcast.10, f32[1,192]{1,0:T(1,128)} %bitcast.11, bf16[3,3,3,192,192]{4,3,2,1,0:T(8,128)(2,1)} %w1_hbm.1, ...), custom_call_target="tpu_custom_call" | custom-call | tf_op jit(solution)/shard_map/pallas_call | solution.py:419
  14.0 0.7 %copy.10 = bf16[1,4,4,6144]{3,2,1,0:T(4,128)(2,1)} copy(bf16[1,4,4,6144]{3,2,1,0:T(4,128)(2,1)S(1)} %bitcast.6) | data formatting | bytes 393216

commit v2 on v1

--- a/solution.py
+++ b/solution.py
@@ -58,7 +58,6 @@
     band = lax.axis_index("space")
     has_prev = tm > 0
     has_next = tm < blocks - 1
-    count = counts_ref[0]
 
     def both(a, b):
         return b if a is None else (a if b is None else jnp.logical_and(a, b))
@@ -121,10 +120,16 @@
     def fill(ref):
         ref[...] = jnp.zeros(ref.shape, ref.dtype)
 
-    pad = jnp.zeros((frames + 2, 1) + p1.shape[2:], BF16)
     if sides == 1:
+        pad = jnp.zeros((frames + 2, 1) + p1.shape[2:], BF16)
         p1[:, 0:1] = pad
         p2[:, 0:1] = pad
+    for plane in (p1, p2):
+        for i in (4, 9):
+            top = plane.shape[1] - 1
+            plane[:, top : top + 1, :, i * LANES : (i + 1) * LANES] = jnp.zeros(
+                (frames + 2, 1, pairs, LANES), BF16
+            )
 
     def no_prev():
         fill(from_time)
@@ -212,11 +217,25 @@
     def after(v):
         return jnp.where(pair < pairs - 1, pltpu.roll(v, pairs - 1, 0), 0.0)
 
-    def put(plane, tiles, frame_at, row_index, with_tiles=True):
+    def put(plane, tiles, frame_at, row_index):
         v0, v1, v2 = tiles
-        mixed = jnp.where(low, after(v1), before(v1))
-        for i, v in enumerate((v0, v1, v2, after(v0), before(v2), mixed)):
-            plane[frame_at, row_index, :, i * LANES : (i + 1) * LANES] = v.astype(BF16)
+        r0, r1, r2 = [pltpu.roll(v, half, 1) for v in tiles]
+        joint = jnp.where(low, r1, r2)
+        nearby = after(v1)
+        even = (before(joint), jnp.where(low, before(r2), r0), jnp.where(low, r0, r1), joint)
+        odd = (v0, v1, v2, after(v0))
+        for n, (values, end, raised) in enumerate(
+            ((even, r2, v2), (odd, nearby, pltpu.roll(nearby, half, 1)))
+        ):
+            at = 5 * n * LANES
+            for i, v in enumerate(values):
+                plane[frame_at, row_index, :, at + i * LANES : at + (i + 1) * LANES] = v.astype(BF16)
+            at += 4 * LANES
+            plane[frame_at, row_index, :, at : at + half] = end[:, :half].astype(BF16)
+            if row_index > 0:
+                plane[frame_at, row_index - 1, :, at + half : at + LANES] = raised[:, half:].astype(
+                    BF16
+                )
 
     def tiles_of(value):
         return [value[:, i * LANES : (i + 1) * LANES] for i in range(3)]
@@ -235,49 +254,45 @@
         return out
 
     def conv(plane, w, frame_at, nf, row_index, nr, taps):
-        even, odd = None, None
-
-        def add(acc, lhs, rhs):
-            term = jnp.dot(lhs, rhs, preferred_element_type=F32)
-            return term if acc is None else acc + term
-
-        rest = LANES - half
+        chains = [None, None]
+        size = nf * nr * pairs
+        done = 0
         zero = jnp.zeros((half, channels), BF16)
-        held = []
+
+        def tile(a, b, i, n):
+            both_columns = []
+            for c in range(2):
+                at = (5 * c + i) * LANES
+                value = plane[
+                    frame_at + a : frame_at + a + nf,
+                    row_index + b : row_index + b + nr,
+                    :,
+                    at : at + n * LANES,
+                ]
+                both_columns.append(value.reshape(size, n * LANES))
+            return jnp.concatenate(both_columns, axis=0)
+
         for a in taps:
+            terms = []
             for b in range(3):
-
-                def tile(i, n=1, a=a, b=b):
-                    value = plane[
-                        frame_at + a : frame_at + a + nf,
-                        row_index + b : row_index + b + nr,
-                        :,
-                        i * LANES : (i + n) * LANES,
-                    ]
-                    return value.reshape(nf * nr * pairs, n * LANES)
-
-                k0, k1, k2 = [w.at[a, b, e] for e in range(3)]
-                main = tile(0, 2)
-                third = tile(2)
-                even = add(even, main, jnp.concatenate([k1[...], k2[:half]], axis=0))
-                odd = add(odd, main, jnp.concatenate([k0[...], k1[:half]], axis=0))
-                even = add(
-                    even,
-                    jnp.concatenate([third, tile(4)], axis=-1),
-                    jnp.concatenate([k2[half:], k0[half:]], axis=0),
+                for n in range(2):
+                    terms.append(
+                        (tile(a, b, 2 * n, 2), w[a, b, 2 * n * LANES : 2 * (n + 1) * LANES])
+                    )
+            ends = [w[a, b, 4 * LANES :] for b in range(3)] + [zero]
+            terms.append(
+                (
+                    jnp.concatenate([tile(a, 0, 4, 1), tile(a, 2, 4, 1)], axis=-1),
+                    jnp.concatenate(ends, axis=0),
                 )
-                odd = add(
-                    odd,
-                    jnp.concatenate([third, tile(3)], axis=-1),
-                    jnp.concatenate([k1[half:], k2[:LANES]], axis=0),
-                )
-                held.append((tile(5), [zero, k0[:half]], [k2[LANES:], zero]))
-                if len(held) == 2 or (a == taps[-1] and b == 2):
-                    lhs = jnp.concatenate([h[0] for h in held], axis=-1)
-                    even = add(even, lhs, jnp.concatenate(sum([h[1] for h in held], []), axis=0))
-                    odd = add(odd, lhs, jnp.concatenate(sum([h[2] for h in held], []), axis=0))
-                    held = []
-        return jnp.concatenate([even, odd], axis=-1)
+            )
+            for lhs, rhs in terms:
+                term = jnp.dot(lhs, rhs, preferred_element_type=F32)
+                n = done % 2
+                chains[n] = term if chains[n] is None else chains[n] + term
+                done += 1
+        a, b = [jnp.concatenate([c[:size], c[size:]], axis=-1) for c in chains]
+        return a + b
 
     def piece(value, n):
         return value[n * pairs : (n + 1) * pairs]
@@ -321,6 +336,7 @@
     def with_input(f, summed):
         return [piece(summed, r) + row_at(own.at[f], r, rows) for r in range(rows)]
 
+    count = counts_ref[0]
     for copy in small:
         copy.wait()
     gain1, bias1, gain2, bias2 = [wide(i) for i in range(4)]
@@ -375,8 +391,11 @@
             frames - 2 + f,
             with_input(frames - 2 + f, summed[f * rows * pairs : (f + 1) * rows * pairs]),
         )
-    for f, taps in ((0, (2,)), (1, (1, 2))):
-        values = with_input(f, conv(p2, w2, f, 1, 0, rows, taps) + bias2)
+    shared = conv(p2, w2, 0, 2, 0, rows, (2,)) + bias2
+    single = conv(p2, w2, 1, 1, 0, rows, (1,))
+    for f in range(2):
+        value = shared[f * rows * pairs : (f + 1) * rows * pairs]
+        values = with_input(f, value + single if f == 1 else value)
         for r in range(rows):
             early[f, r] = values[r]
 
@@ -386,8 +405,11 @@
         for f in range(2):
             for r in range(nr):
                 put(p2, tiles_of(ref[f, r].astype(F32)), f, row + r + 1)
-    for f, taps in ((0, (0, 1)), (1, (0,))):
-        summed = conv(p2, w2, f, 1, 0, rows, taps)
+    shared = conv(p2, w2, 0, 2, 0, rows, (0,))
+    single = conv(p2, w2, 0, 1, 0, rows, (1,))
+    for f in range(2):
+        value = shared[f * rows * pairs : (f + 1) * rows * pairs]
+        summed = value + single if f == 0 else value
         settle(f, [piece(summed, r) + early[f, r] for r in range(rows)])
     for copy, cond in sends + [(c, has_next) for c in hidden_copies]:
         when(cond, copy.wait_send)
@@ -415,6 +437,7 @@
     hbm = pl.BlockSpec(memory_space=pltpu.HBM)
     parts = [rows - 1, 2] if sides == 1 else [rows + 2]
     scratch = pltpu.VMEM
+    taps = (3, 3, 3 * channels, channels)
     rows1 = rows + (3 if sides == 1 else 4)
     out = pl.pallas_call(
         functools.partial(kernel, bands, blocks),
@@ -423,11 +446,11 @@
         out_specs=vmem,
         scratch_shapes=[
             scratch((4, 1, channels), F32),
-            scratch((3, 3, 3, channels, channels), BF16),
-            scratch((3, 3, 3, channels, channels), BF16),
+            scratch((3, 3, 3 * channels, channels), BF16),
+            scratch((3, 3, 3 * channels, channels), BF16),
             scratch(x.shape, BF16),
-            scratch((frames + 2, rows1, pairs, 6 * LANES), BF16),
-            scratch((frames + 2, rows + 2, pairs, 6 * LANES), BF16),
+            scratch((frames + 2, rows1, pairs, 10 * LANES), BF16),
+            scratch((frames + 2, rows + 2, pairs, 10 * LANES), BF16),
             scratch((frames, 3, rows * pairs, LANES), F32),
             scratch((sides, frames, 3, 2 * pairs, LANES), F32),
             scratch((2, 3, rows * pairs, LANES), F32),
@@ -452,8 +475,8 @@
         pltpu.with_memory_space_constraint(bias_first.reshape(1, channels), pltpu.HBM),
         pltpu.with_memory_space_constraint(gain_second.reshape(1, channels), pltpu.HBM),
         pltpu.with_memory_space_constraint(bias_second.reshape(1, channels), pltpu.HBM),
-        pltpu.with_memory_space_constraint(weight_first, pltpu.HBM),
-        pltpu.with_memory_space_constraint(weight_second, pltpu.HBM),
+        pltpu.with_memory_space_constraint(weight_first.reshape(taps), pltpu.HBM),
+        pltpu.with_memory_space_constraint(weight_second.reshape(taps), pltpu.HBM),
     )
     return out.reshape(latents.shape)
 

time: 14.9 us -> 14 us (0.940)
  Pallas kernels: 13.4 us -> 12.5 us
    pallas_call x1, Pallas kernels: 13.4 us -> 12.5 us  [shards(): pl.pallas_call(functools.partial(kernel, bands, blocks), out_shape=pltpu....]
where the time goes in v2:
time: 14 us; the launch traced here: 13.8 us
  Pallas kernels  12.5 us (89%)
  local copies, waits for them, and re-layouts  0.68 us (5%)
  between operations  0.66 us (5%)
    pallas_call x1, Pallas kernels, shards(): pl.pallas_call(functools.partial(kernel, bands, blocks), out_shape=pltpu....  12.5 us
    unnamed x1, local copies, waits for them, and re-layouts  0.68 us

profile of v2, /device:TPU:0, one launch (start us, length us, event | category | flops | bytes accessed | tf_op | source)
XLA Modules:
  0.0 13.8 jit_solution(13179455704546245707)
XLA Ops:
  0.7 12.5 %shard_map.82 = bf16[4,4,6144]{2,1,0:T(4,128)(2,1)S(1)} custom-call(s32[1]{0:T(128)S(6)} %copy.11.counts_ref, bf16[4,4,6144]{2,1,0:T(4,128)(2,1)} %bitcast.11, f32[1,192]{1,0:T(1,128)} %bitcast.12, f32[1,192]{1,0:T(1,128)} %bitcast.13, f32[1,192]{1,0:T(1,128)} %bitcast.14, f32[1,192]{1,0:T(1,128)} %bitcast.15, bf16[3,3,576,192]{3,2,1,0:T(8,128)(2,1)} %bitcast.9, ...), custom_call_target="tpu_custom_call" | custom-call | tf_op jit(solution)/shard_map/pallas_call | solution.py:442
  13.2 0.7 %copy.10 = bf16[1,4,4,6144]{3,2,1,0:T(4,128)(2,1)} copy(bf16[1,4,4,6144]{3,2,1,0:T(4,128)(2,1)S(1)} %bitcast.8) | data formatting | bytes 393216

commit v3 on v2

--- a/solution.py
+++ b/solution.py
@@ -132,10 +132,7 @@
             )
 
     def no_prev():
-        fill(from_time)
-        fill(from_corner)
-        for ref in hidden_in:
-            fill(ref)
+        p1[0:2] = jnp.zeros((2,) + p1.shape[1:], BF16)
 
     pl.when(jnp.logical_not(has_prev))(no_prev)
     if sides == 2:
@@ -151,7 +148,6 @@
             pl.when(jnp.logical_and(jnp.logical_not(slot_cond[slot]), has_prev))(outside_corner)
 
     load_x.wait()
-    pl.semaphore_wait(barrier, total)
 
     def remote(src, dst, at, device):
         return pltpu.make_async_remote_copy(
@@ -178,8 +174,6 @@
             {"tm": tm + 1, "space": peer},
         )
         sends.append((copy, both(cond, has_next)))
-    for copy, cond in sends:
-        when(cond, copy.start)
 
     first = tm * frames
     lane = lax.broadcasted_iota(jnp.int32, (pairs, LANES), 1)
@@ -340,10 +334,6 @@
     for copy in small:
         copy.wait()
     gain1, bias1, gain2, bias2 = [wide(i) for i in range(4)]
-    for f in range(frames):
-        put_rows(x_ref.at[f], rows, own.at[f], f + 2, [(r, r + base1) for r in range(rows)])
-    for copy in loads[0]:
-        copy.wait()
     hidden_copies = []
     if sides == 1:
         parts = [(0, rows - 1), (rows - 1, 2)]
@@ -351,8 +341,20 @@
         parts = [(first_hidden, hrows)]
     for n in range(len(parts)):
         hidden_copies.append(remote(hidden_out[n], hidden_in[n], 5 + n, {"tm": tm + 1}))
+
+    def alone():
+        for f in range(frames):
+            put_rows(x_ref.at[f], rows, own.at[f], f + 2, [(r, r + base1) for r in range(rows)])
+        for copy in loads[0]:
+            copy.wait()
+        if sides == 1:
+            hidden(frames - 2, 2, *parts[0], hidden_out[0])
+
+    pl.semaphore_wait(barrier, total)
+    for copy, cond in sends:
+        when(cond, copy.start)
+    alone()
     if sides == 1:
-        hidden(frames - 2, 2, *parts[0], hidden_out[0])
         when(has_next, hidden_copies[0].start)
 
     def halo_rows(slot):
@@ -361,6 +363,8 @@
         at = 0 if slot == 0 else rows + 2
         return [(0, at), (1, at + 1)]
 
+    if sides == 1:
+        pl.when(jnp.logical_not(has_prev))(lambda: hidden(0, frames - 2, *parts[0]))
     for slot in range(sides):
         landed = remote(
             x_ref.at[:, pl.ds(0, 2)], from_space.at[slot], slot, {"space": band}
@@ -371,18 +375,21 @@
     hidden(frames - 2, 2, *parts[-1], hidden_out[-1])
     when(has_next, hidden_copies[-1].start)
 
-    pl.when(has_prev)(time_copy.wait_recv)
-    for slot in range(sides):
-        landed = remote(
-            x_ref.at[last, pl.ds(0, 2)], from_corner.at[slot], 2 + slot, {"space": band}
-        )
-        when(both(slot_cond[slot], has_prev), landed.wait_recv)
-    for f in range(2):
-        put_rows(from_time.at[f], rows, tail.at[f], f, [(r, r + base1) for r in range(rows)])
+    def from_before():
+        time_copy.wait_recv()
+        for f in range(2):
+            put_rows(from_time.at[f], rows, tail.at[f], f, [(r, r + base1) for r in range(rows)])
         for slot in range(sides):
-            put_rows(from_corner.at[slot, f], 2, corner.at[slot, f], f, halo_rows(slot))
-
-    hidden(0, frames - 2, first_hidden, hrows)
+            landed = remote(
+                x_ref.at[last, pl.ds(0, 2)], from_corner.at[slot], 2 + slot, {"space": band}
+            )
+            when(slot_cond[slot], landed.wait_recv)
+            for f in range(2):
+                put_rows(from_corner.at[slot, f], 2, corner.at[slot, f], f, halo_rows(slot))
+        hidden(0, frames - 2, first_hidden, hrows)
+
+    pl.when(has_prev)(from_before)
+    pl.when(jnp.logical_not(has_prev))(lambda: hidden(0, frames - 2, *parts[-1]))
     for copy in loads[1]:
         copy.wait()
     summed = conv(p2, w2, frames - 2, 2, 0, rows, (0, 1, 2)) + bias2
@@ -399,18 +406,25 @@
         for r in range(rows):
             early[f, r] = values[r]
 
-    for copy in hidden_copies:
-        pl.when(has_prev)(copy.wait_recv)
-    for (row, nr), ref in zip(parts, hidden_in):
+    def add_before():
+        for (row, nr), ref, copy in zip(parts, hidden_in, hidden_copies):
+            copy.wait_recv()
+            for f in range(2):
+                for r in range(nr):
+                    put(p2, tiles_of(ref[f, r].astype(F32)), f, row + r + 1)
+        shared = conv(p2, w2, 0, 2, 0, rows, (0,))
+        single = conv(p2, w2, 0, 1, 0, rows, (1,))
         for f in range(2):
-            for r in range(nr):
-                put(p2, tiles_of(ref[f, r].astype(F32)), f, row + r + 1)
-    shared = conv(p2, w2, 0, 2, 0, rows, (0,))
-    single = conv(p2, w2, 0, 1, 0, rows, (1,))
-    for f in range(2):
-        value = shared[f * rows * pairs : (f + 1) * rows * pairs]
-        summed = value + single if f == 0 else value
-        settle(f, [piece(summed, r) + early[f, r] for r in range(rows)])
+            value = shared[f * rows * pairs : (f + 1) * rows * pairs]
+            summed = value + single if f == 0 else value
+            settle(f, [piece(summed, r) + early[f, r] for r in range(rows)])
+
+    def without_before():
+        for f in range(2):
+            settle(f, [early[f, r] for r in range(rows)])
+
+    pl.when(has_prev)(add_before)
+    pl.when(jnp.logical_not(has_prev))(without_before)
     for copy, cond in sends + [(c, has_next) for c in hidden_copies]:
         when(cond, copy.wait_send)
 

time: 14 us -> 13.3 us (0.950)
  the two profiles are of different devices: /device:TPU:0 before, /device:TPU:14 now
where the time goes in v3:
time: 13.3 us; the launch traced here: 13.1 us
  Pallas kernels  11.7 us (88%)
  local copies, waits for them, and re-layouts  0.68 us (5%)
  between operations  0.66 us (5%)
    pallas_call x1, Pallas kernels, shards(): pl.pallas_call(functools.partial(kernel, bands, blocks), out_shape=pltpu....  11.7 us
    unnamed x1, local copies, waits for them, and re-layouts  0.68 us

profile of v3, /device:TPU:14, one launch (start us, length us, event | category | flops | bytes accessed | tf_op | source)
XLA Modules:
  0.0 13.1 jit_solution(2049783814524137807)
XLA Ops:
  0.7 11.7 %shard_map.82 = bf16[4,4,6144]{2,1,0:T(4,128)(2,1)S(1)} custom-call(s32[1]{0:T(128)S(6)} %copy.11.counts_ref, bf16[4,4,6144]{2,1,0:T(4,128)(2,1)} %bitcast.11, f32[1,192]{1,0:T(1,128)} %bitcast.12, f32[1,192]{1,0:T(1,128)} %bitcast.13, f32[1,192]{1,0:T(1,128)} %bitcast.14, f32[1,192]{1,0:T(1,128)} %bitcast.15, bf16[3,3,576,192]{3,2,1,0:T(8,128)(2,1)} %bitcast.9, ...), custom_call_target="tpu_custom_call" | custom-call | tf_op jit(solution)/shard_map/pallas_call | solution.py:456
  12.4 0.7 %copy.10 = bf16[1,4,4,6144]{3,2,1,0:T(4,128)(2,1)} copy(bf16[1,4,4,6144]{3,2,1,0:T(4,128)(2,1)S(1)} %bitcast.8) | data formatting | bytes 393216

commit v4 on v3

--- a/solution.py
+++ b/solution.py
@@ -342,19 +342,15 @@
     for n in range(len(parts)):
         hidden_copies.append(remote(hidden_out[n], hidden_in[n], 5 + n, {"tm": tm + 1}))
 
-    def alone():
-        for f in range(frames):
-            put_rows(x_ref.at[f], rows, own.at[f], f + 2, [(r, r + base1) for r in range(rows)])
-        for copy in loads[0]:
-            copy.wait()
-        if sides == 1:
-            hidden(frames - 2, 2, *parts[0], hidden_out[0])
-
     pl.semaphore_wait(barrier, total)
     for copy, cond in sends:
         when(cond, copy.start)
-    alone()
+    for copy in loads[0]:
+        copy.wait()
+    for f in range(frames):
+        put_rows(x_ref.at[f], rows, own.at[f], f + 2, [(r, r + base1) for r in range(rows)])
     if sides == 1:
+        hidden(frames - 2, 2, *parts[0], hidden_out[0])
         when(has_next, hidden_copies[0].start)
 
     def halo_rows(slot):
@@ -375,43 +371,47 @@
     hidden(frames - 2, 2, *parts[-1], hidden_out[-1])
     when(has_next, hidden_copies[-1].start)
 
+    def finish():
+        for f in range(frames - 2, frames):
+            settle(f, with_input(f, conv(p2, w2, f, 1, 0, rows, (0, 1, 2)) + bias2))
+
+    def start_first():
+        shared = conv(p2, w2, 0, 2, 0, rows, (2,)) + bias2
+        single = conv(p2, w2, 1, 1, 0, rows, (1,))
+        values = []
+        for f in range(2):
+            value = shared[f * rows * pairs : (f + 1) * rows * pairs]
+            values.append(with_input(f, value + single if f == 1 else value))
+        return values
+
+    def fetch(n):
+        (row, nr), ref = parts[n], hidden_in[n]
+        hidden_copies[n].wait_recv()
+        for f in range(2):
+            for r in range(nr):
+                put(p2, tiles_of(ref[f, r].astype(F32)), f, row + r + 1)
+
     def from_before():
         time_copy.wait_recv()
-        for f in range(2):
-            put_rows(from_time.at[f], rows, tail.at[f], f, [(r, r + base1) for r in range(rows)])
         for slot in range(sides):
             landed = remote(
                 x_ref.at[last, pl.ds(0, 2)], from_corner.at[slot], 2 + slot, {"space": band}
             )
             when(slot_cond[slot], landed.wait_recv)
-            for f in range(2):
+        for f in range(2):
+            put_rows(from_time.at[f], rows, tail.at[f], f, [(r, r + base1) for r in range(rows)])
+            for slot in range(sides):
                 put_rows(from_corner.at[slot, f], 2, corner.at[slot, f], f, halo_rows(slot))
-        hidden(0, frames - 2, first_hidden, hrows)
-
-    pl.when(has_prev)(from_before)
-    pl.when(jnp.logical_not(has_prev))(lambda: hidden(0, frames - 2, *parts[-1]))
-    for copy in loads[1]:
-        copy.wait()
-    summed = conv(p2, w2, frames - 2, 2, 0, rows, (0, 1, 2)) + bias2
-    for f in range(2):
-        settle(
-            frames - 2 + f,
-            with_input(frames - 2 + f, summed[f * rows * pairs : (f + 1) * rows * pairs]),
-        )
-    shared = conv(p2, w2, 0, 2, 0, rows, (2,)) + bias2
-    single = conv(p2, w2, 1, 1, 0, rows, (1,))
-    for f in range(2):
-        value = shared[f * rows * pairs : (f + 1) * rows * pairs]
-        values = with_input(f, value + single if f == 1 else value)
-        for r in range(rows):
-            early[f, r] = values[r]
-
-    def add_before():
-        for (row, nr), ref, copy in zip(parts, hidden_in, hidden_copies):
-            copy.wait_recv()
-            for f in range(2):
-                for r in range(nr):
-                    put(p2, tiles_of(ref[f, r].astype(F32)), f, row + r + 1)
+        for f in range(frames - 2):
+            hidden(f, 1, first_hidden, hrows)
+        if sides == 1:
+            fetch(0)
+        finish()
+        values = start_first()
+        for f in range(2):
+            for r in range(rows):
+                early[f, r] = values[f][r]
+        fetch(len(parts) - 1)
         shared = conv(p2, w2, 0, 2, 0, rows, (0,))
         single = conv(p2, w2, 0, 1, 0, rows, (1,))
         for f in range(2):
@@ -420,10 +420,15 @@
             settle(f, [piece(summed, r) + early[f, r] for r in range(rows)])
 
     def without_before():
+        hidden(0, frames - 2, *parts[-1])
+        finish()
+        values = start_first()
         for f in range(2):
-            settle(f, [early[f, r] for r in range(rows)])
-
-    pl.when(has_prev)(add_before)
+            settle(f, values[f])
+
+    for copy in loads[1]:
+        copy.wait()
+    pl.when(has_prev)(from_before)
     pl.when(jnp.logical_not(has_prev))(without_before)
     for copy, cond in sends + [(c, has_next) for c in hidden_copies]:
         when(cond, copy.wait_send)

time: 13.3 us -> 13.2 us (level)
  no operation moved by 1% of the time
where the time goes in v4:
time: 13.2 us; the launch traced here: 13 us
  Pallas kernels  11.7 us (89%)
  local copies, waits for them, and re-layouts  0.68 us (5%)
  between operations  0.66 us (5%)
    pallas_call x1, Pallas kernels, shards(): pl.pallas_call(functools.partial(kernel, bands, blocks), out_shape=pltpu....  11.7 us
    unnamed x1, local copies, waits for them, and re-layouts  0.68 us

profile of v4, /device:TPU:14, one launch (start us, length us, event | category | flops | bytes accessed | tf_op | source)
XLA Modules:
  0.0 13.0 jit_solution(7881512874214953229)
XLA Ops:
  0.7 11.7 %shard_map.82 = bf16[4,4,6144]{2,1,0:T(4,128)(2,1)S(1)} custom-call(s32[1]{0:T(128)S(6)} %copy.11.counts_ref, bf16[4,4,6144]{2,1,0:T(4,128)(2,1)} %bitcast.11, f32[1,192]{1,0:T(1,128)} %bitcast.12, f32[1,192]{1,0:T(1,128)} %bitcast.13, f32[1,192]{1,0:T(1,128)} %bitcast.14, f32[1,192]{1,0:T(1,128)} %bitcast.15, bf16[3,3,576,192]{3,2,1,0:T(8,128)(2,1)} %bitcast.9, ...), custom_call_target="tpu_custom_call" | custom-call | tf_op jit(solution)/shard_map/pallas_call | solution.py:461
  12.3 0.7 %copy.10 = bf16[1,4,4,6144]{3,2,1,0:T(4,128)(2,1)} copy(bf16[1,4,4,6144]{3,2,1,0:T(4,128)(2,1)S(1)} %bitcast.8) | data formatting | bytes 393216

commit v5 on v4

--- a/solution.py
+++ b/solution.py
@@ -36,6 +36,7 @@
     tail,
     corner,
     early,
+    begun,
     from_time,
     from_space,
     from_corner,
@@ -247,7 +248,7 @@
             out.append(scaled * jax.nn.sigmoid(scaled))
         return out
 
-    def conv(plane, w, frame_at, nf, row_index, nr, taps):
+    def conv(plane, w, frame_at, nf, row_index, nr, taps, across=(0, 1, 2), end=True):
         chains = [None, None]
         size = nf * nr * pairs
         done = 0
@@ -268,18 +269,19 @@
 
         for a in taps:
             terms = []
-            for b in range(3):
+            for b in across:
                 for n in range(2):
                     terms.append(
                         (tile(a, b, 2 * n, 2), w[a, b, 2 * n * LANES : 2 * (n + 1) * LANES])
                     )
-            ends = [w[a, b, 4 * LANES :] for b in range(3)] + [zero]
-            terms.append(
-                (
-                    jnp.concatenate([tile(a, 0, 4, 1), tile(a, 2, 4, 1)], axis=-1),
-                    jnp.concatenate(ends, axis=0),
+            if end:
+                ends = [w[a, b, 4 * LANES :] for b in range(3)] + [zero]
+                terms.append(
+                    (
+                        jnp.concatenate([tile(a, 0, 4, 1), tile(a, 2, 4, 1)], axis=-1),
+                        jnp.concatenate(ends, axis=0),
+                    )
                 )
-            )
             for lhs, rhs in terms:
                 term = jnp.dot(lhs, rhs, preferred_element_type=F32)
                 n = done % 2
@@ -297,8 +299,26 @@
         for row, row_index in row_list:
             put(p1, norm(row_at(target, row, rows_in), scale), frame_at, row_index)
 
-    def hidden(frame_at, nf, row, nr, saved=None):
-        summed = conv(p1, w1, frame_at, nf, row - 1 + base1, nr, (0, 1, 2)) + bias1
+    def beside(frame_at, nf, row):
+        at = row - 1 + base1
+        lower = conv(p1, w1, frame_at, nf, at, 2, (0, 1, 2), (0,), False)
+        own_row = conv(p1, w1, frame_at, nf, at, 1, (0, 1, 2), (1,), False)
+        for f in range(nf):
+            begun[f, 0] = piece(lower, 2 * f) + piece(own_row, f)
+            begun[f, 1] = piece(lower, 2 * f + 1)
+
+    def hidden(frame_at, nf, row, nr, saved=None, rest=False):
+        at = row - 1 + base1
+        if rest:
+            upper = conv(p1, w1, frame_at, nf, at, 2, (0, 1, 2), (2,))
+            last_row = conv(p1, w1, frame_at, nf, at + 1, 1, (0, 1, 2), (1,), False)
+            values = []
+            for f in range(nf):
+                values.append(piece(upper, 2 * f) + begun[f, 0])
+                values.append(piece(upper, 2 * f + 1) + piece(last_row, f) + begun[f, 1])
+            summed = jnp.concatenate(values, axis=0) + bias1
+        else:
+            summed = conv(p1, w1, frame_at, nf, at, nr, (0, 1, 2)) + bias1
         rounded = summed.astype(BF16).astype(F32)
         for f in range(nf):
             scale = scale_of(gain2, frame_at + f + 2)
@@ -352,6 +372,7 @@
     if sides == 1:
         hidden(frames - 2, 2, *parts[0], hidden_out[0])
         when(has_next, hidden_copies[0].start)
+        beside(frames - 2, 2, parts[1][0])
 
     def halo_rows(slot):
         if sides == 1:
@@ -361,6 +382,8 @@
 
     if sides == 1:
         pl.when(jnp.logical_not(has_prev))(lambda: hidden(0, frames - 2, *parts[0]))
+    for copy in loads[1]:
+        copy.wait()
     for slot in range(sides):
         landed = remote(
             x_ref.at[:, pl.ds(0, 2)], from_space.at[slot], slot, {"space": band}
@@ -368,12 +391,29 @@
         when(slot_cond[slot], landed.wait_recv)
         for f in range(frames):
             put_rows(from_space.at[slot, f], 2, halo.at[slot, f], f + 2, halo_rows(slot))
-    hidden(frames - 2, 2, *parts[-1], hidden_out[-1])
-    when(has_next, hidden_copies[-1].start)
+    hidden(frames - 2, 2, *parts[-1], None, sides == 1)
+    out_row, out_rows = (rows - 2, 2) if sides == 1 else (0, rows)
+
+    def forward():
+        shared = conv(p2, w2, frames, 2, out_row, out_rows, (0,))
+        single = conv(p2, w2, frames, 1, out_row, out_rows, (1,))
+        for f in range(2):
+            for r in range(out_rows):
+                value = piece(shared, f * out_rows + r)
+                value = value + piece(single, r) if f == 0 else value
+                for i, v in enumerate(tiles_of(value)):
+                    hidden_out[-1][f, r, :, i * LANES : (i + 1) * LANES] = v.astype(BF16)
+        hidden_copies[-1].start()
+
+    pl.when(has_next)(forward)
 
     def finish():
-        for f in range(frames - 2, frames):
-            settle(f, with_input(f, conv(p2, w2, f, 1, 0, rows, (0, 1, 2)) + bias2))
+        summed = conv(p2, w2, frames - 2, 2, 0, rows, (0, 1, 2)) + bias2
+        for f in range(2):
+            settle(
+                frames - 2 + f,
+                with_input(frames - 2 + f, summed[f * rows * pairs : (f + 1) * rows * pairs]),
+            )
 
     def start_first():
         shared = conv(p2, w2, 0, 2, 0, rows, (2,)) + bias2
@@ -408,16 +448,22 @@
             fetch(0)
         finish()
         values = start_first()
+        if sides == 1:
+            shared = conv(p2, w2, 0, 2, 0, out_row, (0,))
+            single = conv(p2, w2, 0, 1, 0, out_row, (1,))
+            for r in range(out_row):
+                values[0][r] = values[0][r] + piece(shared, r) + piece(single, r)
+                values[1][r] = values[1][r] + piece(shared, out_row + r)
         for f in range(2):
             for r in range(rows):
                 early[f, r] = values[f][r]
-        fetch(len(parts) - 1)
-        shared = conv(p2, w2, 0, 2, 0, rows, (0,))
-        single = conv(p2, w2, 0, 1, 0, rows, (1,))
-        for f in range(2):
-            value = shared[f * rows * pairs : (f + 1) * rows * pairs]
-            summed = value + single if f == 0 else value
-            settle(f, [piece(summed, r) + early[f, r] for r in range(rows)])
+        hidden_copies[-1].wait_recv()
+        for f in range(2):
+            values = [early[f, r] for r in range(rows)]
+            for r in range(out_rows):
+                at = out_row + r
+                values[at] = values[at] + hidden_in[-1][f, r].astype(F32)
+            settle(f, values)
 
     def without_before():
         hidden(0, frames - 2, *parts[-1])
@@ -426,8 +472,6 @@
         for f in range(2):
             settle(f, values[f])
 
-    for copy in loads[1]:
-        copy.wait()
     pl.when(has_prev)(from_before)
     pl.when(jnp.logical_not(has_prev))(without_before)
     for copy, cond in sends + [(c, has_next) for c in hidden_copies]:
@@ -454,7 +498,7 @@
     sides = 1 if bands == 2 else 2
     vmem = pl.BlockSpec(memory_space=pltpu.VMEM)
     hbm = pl.BlockSpec(memory_space=pltpu.HBM)
-    parts = [rows - 1, 2] if sides == 1 else [rows + 2]
+    parts = [rows - 1, 2] if sides == 1 else [rows]
     scratch = pltpu.VMEM
     taps = (3, 3, 3 * channels, channels)
     rows1 = rows + (3 if sides == 1 else 4)
@@ -475,6 +519,7 @@
             scratch((2, 3, rows * pairs, LANES), F32),
             scratch((sides, 2, 3, 2 * pairs, LANES), F32),
             scratch((2, rows, pairs, flat), F32),
+            scratch((2, 2, pairs, flat), F32),
             scratch((2, rows, width), BF16),
             scratch((sides, frames, 2, width), BF16),
             scratch((sides, 2, 2, width), BF16),

time: 13.2 us -> 12.8 us (0.970)
  Pallas kernels: 11.7 us -> 11.3 us
    pallas_call x1, Pallas kernels: 11.7 us -> 11.3 us  [shards(): pl.pallas_call(functools.partial(kernel, bands, blocks), out_shape=pltpu....]
where the time goes in v5:
time: 12.8 us; the launch traced here: 12.7 us
  Pallas kernels  11.3 us (88%)
  local copies, waits for them, and re-layouts  0.68 us (5%)
  between operations  0.66 us (5%)
    pallas_call x1, Pallas kernels, shards(): pl.pallas_call(functools.partial(kernel, bands, blocks), out_shape=pltpu....  11.3 us
    unnamed x1, local copies, waits for them, and re-layouts  0.68 us

profile of v5, /device:TPU:14, one launch (start us, length us, event | category | flops | bytes accessed | tf_op | source)
XLA Modules:
  0.0 12.7 jit_solution(12707571277016822115)
XLA Ops:
  0.7 11.3 %shard_map.82 = bf16[4,4,6144]{2,1,0:T(4,128)(2,1)S(1)} custom-call(s32[1]{0:T(128)S(6)} %copy.11.counts_ref, bf16[4,4,6144]{2,1,0:T(4,128)(2,1)} %bitcast.11, f32[1,192]{1,0:T(1,128)} %bitcast.12, f32[1,192]{1,0:T(1,128)} %bitcast.13, f32[1,192]{1,0:T(1,128)} %bitcast.14, f32[1,192]{1,0:T(1,128)} %bitcast.15, bf16[3,3,576,192]{3,2,1,0:T(8,128)(2,1)} %bitcast.9, ...), custom_call_target="tpu_custom_call" | custom-call | tf_op jit(solution)/shard_map/pallas_call | solution.py:505
  12.0 0.7 %copy.10 = bf16[1,4,4,6144]{3,2,1,0:T(4,128)(2,1)} copy(bf16[1,4,4,6144]{3,2,1,0:T(4,128)(2,1)S(1)} %bitcast.8) | data formatting | bytes 393216
